TPU v7x, 512 devices: a whole 4x4x16 slice. The times are simulated.
512 devices in a mesh: dp: 2 (over core), fsdp: 32 (over y, z_lo), tensor: 8 (over z_hi, x).
Axes of the slice: x: 4, y: 4, z: 16 (z_hi: 2, z_lo: 8; z = z_hi * 8 + z_lo), core: 2. Of those that a mesh axis runs over, the one named last changes fastest.
Arguments:
- tokens: bfloat16 [16384, 4096], P(('dp', 'fsdp', 'tensor')), may hold values from -40 to 40
- norm_gain: float32 [4096], replicated, may hold values from 0.5 to 1.5
- tile_values: bfloat16 [512, 128, 128], P(('fsdp', 'tensor')), may hold values from -0.25 to 0.25
- tile_rows: int32 [8, 64], P('tensor'), may hold values from 0 to 31, as said below
- tile_cols: int32 [8, 64], P('tensor'), may hold values from 0 to 13
- tile_counts: int32 [8, 32], P('tensor'), may hold values from 0 to 2, as said below
- grad_out: bfloat16 [16384, 14336], P(('dp', 'fsdp'), 'tensor'), may hold values from -3 to 3
Outputs:
- mixed: bfloat16 [16384, 14336], P(('dp', 'fsdp'), 'tensor')
- grad_x: bfloat16 [16384, 4096], P(('dp', 'fsdp', 'tensor'))
- grad_gain: float32 [4096], replicated
- grad_tiles: float32 [512, 128, 128], P(('fsdp', 'tensor'))
Inputs may be any that keep to these rules, and one draw needn't show every extreme that they name: `tile_counts`: for each tensor index the counts over the 32 fsdp shards sum to 56, and some shard holds exactly 2. `tile_rows`: within one tensor index the (row, column) pairs of held slots are all different.
All inputs are finite; a program needn't handle non-finite values.
Results may differ from a plain program's by a relative error of at most 0.013.
Values may be sent and summed in bfloat16 or wider, within the bound.
A program may use at most 128 MiB of HBM per device.

v0:
```python
import jax
import jax.numpy as jnp
from jax import lax
from jax.sharding import PartitionSpec as P


def tile_forward(group_rows, values, rows_list, cols_list, col_tiles):
    tile_size = values.shape[1]
    blocks = group_rows.reshape(group_rows.shape[0], -1, tile_size)
    picked = jnp.take(blocks, rows_list, axis=1)
    product = jnp.einsum("tsk,skn->tsn", picked, values, preferred_element_type=jnp.float32)
    placed = (
        jnp.zeros((group_rows.shape[0], col_tiles, tile_size), jnp.float32)
        .at[:, cols_list]
        .add(product)
    )
    return placed.reshape(group_rows.shape[0], col_tiles * tile_size)


def tile_backward(grad_rows, values, rows_list, cols_list, row_tiles):
    tile_size = values.shape[1]
    blocks = grad_rows.reshape(grad_rows.shape[0], -1, tile_size)
    picked = jnp.take(blocks, cols_list, axis=1)
    product = jnp.einsum("tsn,skn->tsk", picked, values, preferred_element_type=jnp.float32)
    placed = (
        jnp.zeros((grad_rows.shape[0], row_tiles, tile_size), jnp.float32)
        .at[:, rows_list]
        .add(product)
    )
    return placed.reshape(grad_rows.shape[0], row_tiles * tile_size)


def per_device(tokens, norm_gain, tile_values, tile_rows, tile_cols, tile_counts, grad_out):
    tile_size = tile_values.shape[1]
    slot_cap = tile_values.shape[0]
    row_tiles = tokens.shape[1] // tile_size
    col_tiles = grad_out.shape[1] // tile_size
    rows_list = tile_rows[0]
    cols_list = tile_cols[0]
    shard_counts = tile_counts[0]
    held_all = (jnp.arange(slot_cap)[None, :] < shard_counts[:, None]).reshape(-1)
    own_held = jnp.arange(slot_cap) < shard_counts[lax.axis_index("fsdp")]
    local_float = tokens.astype(jnp.float32)
    inv_rms = lax.rsqrt(jnp.mean(local_float * local_float, axis=1, keepdims=True) + 1e-05)
    scaled = local_float * inv_rms
    normed = (scaled * norm_gain).astype(jnp.bfloat16)
    group_rows = lax.all_gather(normed, "tensor", axis=0, tiled=True)
    gathered = lax.all_gather(tile_values, "fsdp", axis=0, tiled=True)
    kept_values = jnp.where(held_all[:, None, None], gathered, jnp.zeros_like(gathered))
    outputs = tile_forward(group_rows, kept_values, rows_list, cols_list, col_tiles)
    mixed = outputs.astype(jnp.bfloat16)
    input_grad = lax.psum_scatter(
        tile_backward(grad_out, kept_values, rows_list, cols_list, row_tiles).astype(jnp.bfloat16),
        "tensor",
        scatter_dimension=0,
        tiled=True,
    ).astype(jnp.float32)
    x_blocks = group_rows.reshape(group_rows.shape[0], row_tiles, tile_size)
    g_blocks = grad_out.reshape(grad_out.shape[0], col_tiles, tile_size)
    picked_x = jnp.take(x_blocks, rows_list, axis=1)
    picked_g = jnp.take(g_blocks, cols_list, axis=1)
    grad_shard = lax.psum_scatter(
        jnp.einsum("tsk,tsn->skn", picked_x, picked_g, preferred_element_type=jnp.float32),
        "fsdp",
        scatter_dimension=0,
        tiled=True,
    )
    grad_shard = jnp.where(own_held[:, None, None], grad_shard, jnp.zeros_like(grad_shard))
    grad_tiles = lax.psum(grad_shard, "dp")
    gain_part = jnp.sum(input_grad * scaled, axis=0)
    grad_gain = lax.psum(gain_part, ("dp", "fsdp", "tensor"))
    hidden_grad = input_grad * norm_gain
    grad_x = (
        inv_rms * (hidden_grad - scaled * jnp.mean(hidden_grad * scaled, axis=1, keepdims=True))
    ).astype(jnp.bfloat16)
    return (mixed, grad_x, grad_gain, grad_tiles)


def solution(mesh):
    placed = (
        P(("dp", "fsdp", "tensor"), None),
        P(),
        P(("fsdp", "tensor"), None, None),
        P("tensor", None),
        P("tensor", None),
        P("tensor", None),
        P(("dp", "fsdp"), "tensor"),
    )
    return jax.shard_map(
        per_device,
        mesh=mesh,
        in_specs=placed,
        out_specs=(
            P(("dp", "fsdp"), "tensor"),
            P(("dp", "fsdp", "tensor"), None),
            P(),
            P(("fsdp", "tensor"), None, None),
        ),
        check_vma=False,
    )
```

profile of v0, /device:TPU:1, one launch (start us, length us, event | category | flops | bytes accessed | tf_op | source)
XLA Modules:
  0.0 848.5 jit_solution(9026113694259479338)
XLA Ops:
  7.2 0.0 all-gather.3.cloned.1.call-start
  7.2 0.7 all-gather.3.cloned.1.call-update
  7.9 0.0 reduce-scatter.7.cloned.1.call-start
  7.9 1.5 copy.32
  9.4 0.6 copy.33
  10.0 0.7 iota_compare_fusion
  10.8 0.1 lt.72
  10.9 0.7 compare_select_fusion
  11.6 0.0 copy-start.4
  11.6 0.0 copy-start.5
  11.6 3.1 gather_fusion.1
  14.6 0.0 copy-done.4
  14.6 0.0 copy-done.5
  14.7 207.7 %all-gather.3.cloned.1.call-done = bf16[64,128,128]{2,1,0:T(8,128)(2,1)} async-done(((bf16[2,128,128]{2,1,0:T(8,128)(2,1)}), bf16[64,128,128]{2,1,0:T(8,128)(2,1)}) %all-gather.3.cloned.1.call-update) | async-done | bytes 2097168 | tf_op jit(solution)/shard_map/all_gather | solution.py:48
  222.3 7.4 fusion.2
  229.8 2.4 broadcast_in_dim.57
  232.2 19.4 %scatter_fusion.1 = f32[256,32,128]{2,0,1:T(8,128)} fusion(f32[256,32,128]{2,0,1:T(8,128)} %broadcast_in_dim.57, s32[64]{0:T(128)S(1)} %fusion.18, f32[64,256,128]{2,1,0:T(8,128)} %fusion.2), kind=kCustom, calls=%fused_computation.3 | custom fusion | flops 2097152 | bytes 25166080 | tf_op jit(solution)/shard_map/scatter-add | solution.py:28
  251.6 2.5 convert_element_type.28
  254.1 2.9 copy.34
  257.0 0.0 copy-start.1
  257.0 0.0 copy-start.2
  257.0 4.1 copy.39
  261.2 0.0 reduce-scatter.7.cloned.1.call-update
  261.2 0.0 all-gather.5.cloned.1.call-start
  261.2 0.0 copy-done.1
  261.2 0.2 fusion.15
  261.4 162.8 %reduce-scatter.7.cloned.1.call-done = bf16[32,4096]{1,0:T(8,128)(2,1)} async-done(((bf16[256,4096]{1,0:T(8,128)(2,1)}), bf16[32,4096]{1,0:T(8,128)(2,1)}) %reduce-scatter.7.cloned.1.call-update) | async-done | bytes 262160 | tf_op jit(solution)/shard_map/reduce_scatter | solution.py:52
  424.3 0.0 copy-done.2
  424.3 1.3 fusion.16
  425.5 1.9 fusion.12
  427.5 0.0 all-gather.5.cloned.1.call-update
  427.5 0.0 reduce-scatter.5.cloned.1.call-start
  427.6 109.9 %all-gather.5.cloned.1.call-done = bf16[256,4096]{1,0:T(8,128)(2,1)} async-done(((bf16[32,4096]{1,0:T(8,128)(2,1)}), bf16[256,4096]{1,0:T(8,128)(2,1)}) %all-gather.5.cloned.1.call-update) | async-done | bytes 2097168 | tf_op jit(solution)/shard_map/all_gather | solution.py:47
  537.5 4.1 copy.29
  541.6 3.2 copy.30
  544.8 3.0 gather_fusion
  547.8 7.0 fusion
  554.8 0.0 copy-start.3
  554.8 0.0 copy-start
  554.8 0.0 reduce-scatter.5.cloned.1.call-update
  554.9 0.0 all-reduce.2.cloned.1.call-start
  554.9 0.6 copy-done.3
  555.5 0.6 constant_dynamic-slice_fusion
  556.1 0.6 iota_compare_fusion.1
  556.7 103.2 %psum.14 = f32[4096]{0:T(1024)} all-reduce(f32[4096]{0:T(1024)S(1)} %get-tuple-element.18), channel_id=1, replica_groups=mesh['dp'=2,'fsdp'=32,'tensor'=8] {'dp','fsdp','tensor'}, use_global_device_ids=true, to_apply=%region_6.9 | all-reduce | flops 4096 | bytes 32768 | tf_op jit(solution)/shard_map/psum | solution.py:71
  659.9 119.5 %reduce-scatter.5.cloned.1.call-done = f32[2,128,128]{2,1,0:T(8,128)} async-done(((f32[64,128,128]{2,1,0:T(8,128)}), f32[2,128,128]{2,1,0:T(8,128)}) %reduce-scatter.5.cloned.1.call-update) | async-done | bytes 131088 | tf_op jit(solution)/shard_map/reduce_scatter | solution.py:62
  779.5 1.6 broadcast_select_fusion.9
  781.1 0.0 all-reduce.2.cloned.1.call-update
  781.1 0.0 copy-done
  781.1 6.7 fusion.5
  787.9 0.2 broadcast_in_dim.54
  788.0 12.4 %scatter_fusion = f32[256,14,128]{2,0,1:T(8,128)S(1)} fusion(f32[256,14,128]{2,0,1:T(8,128)S(1)} %broadcast_in_dim.54, s32[64]{0:T(128)S(1)} %fusion.17, f32[64,256,128]{2,1,0:T(8,128)} %fusion.5), kind=kCustom, calls=%fused_computation.2 | custom fusion | flops 2097152 | bytes 25166080 | tf_op jit(solution)/shard_map/scatter-add | solution.py:15
  800.5 0.2 convert_element_type.26
  800.6 0.5 copy.31
  801.2 1.4 copy.37
  802.5 37.8 %all-reduce.2.cloned.1.call-done = f32[2,128,128]{2,1,0:T(8,128)} async-done(((f32[2,128,128]{2,1,0:T(8,128)}), f32[2,128,128]{2,1,0:T(8,128)}) %all-reduce.2.cloned.1.call-update) | async-done | bytes 131088 | tf_op jit(solution)/shard_map/psum | solution.py:69
  840.4 1.6 copy.44
  (8 shorter events, 0.0 us)
Async XLA Ops:
  7.2 215.2 %all-gather.3.cloned.1.call-start = ((), (), s32[]{:S(2)}) async-start(), calls=%async_computation.2 | async-start | bytes 2162688 | tf_op jit(solution)/shard_map/all_gather | solution.py:48
  7.9 416.4 %reduce-scatter.7.cloned.1.call-start = ((), (), s32[]{:S(2)}) async-start(), calls=%async_computation.6 | async-start | bytes 2359296 | tf_op jit(solution)/shard_map/reduce_scatter | solution.py:52
  11.6 3.1 copy-start.4
  11.6 3.1 copy-start.5
  257.0 4.2 copy-start.1
  257.0 167.2 %copy-start.2 = (f32[4096]{0:T(1024)S(1)}, f32[4096]{0:T(1024)}, u32[]{:S(2)}) copy-start(f32[4096]{0:T(1024)} %param.12) | copy-start | bytes 49156
  261.2 276.3 %all-gather.5.cloned.1.call-start = ((), (), s32[]{:S(2)}) async-start(), calls=%async_computation.3 | async-start | bytes 2359296 | tf_op jit(solution)/shard_map/all_gather | solution.py:47
  427.5 352.0 %reduce-scatter.5.cloned.1.call-start = ((), (), s32[]{:S(2)}) async-start(), calls=%async_computation.4 | async-start | bytes 4325376 | tf_op jit(solution)/shard_map/reduce_scatter | solution.py:62
  554.8 0.7 copy-start.3
  554.8 226.3 %copy-start = (bf16[64,128,128]{2,1,0:T(8,128)(2,1)S(1)}, bf16[64,128,128]{2,1,0:T(8,128)(2,1)}, u32[]{:S(2)}) copy-start(bf16[64,128,128]{2,1,0:T(8,128)(2,1)} %all-gather.3.cloned.1.call-done) | copy-start | bytes 6291460
  554.9 285.5 %all-reduce.2.cloned.1.call-start = ((), (), s32[]{:S(2)}) async-start(), calls=%async_computation.5 | async-start | bytes 262144 | tf_op jit(solution)/shard_map/psum | solution.py:69
Sparse Core Ops, SparseCore 0:
  10.1 212.2 all-gather.2
  261.3 162.8 reduce-scatter.6
  428.5 108.9 all-gather.4
  555.0 224.4 reduce-scatter.4
  783.0 57.3 all-reduce.1
where the time goes:
time: 849 us; the launch traced here: 848 us
  waiting for transfers between devices  639 us (75%)
  blocking collectives  103 us (12%)
  other arithmetic  41.6 us (5%)
  local copies, waits for them, and re-layouts  29.9 us (4%)
  matrix products  21.2 us (2%)
  between operations  13.9 us (2%)
    all_gather x1, waiting for transfers between devices, per_device(): gathered = lax.all_gather(tile_values, 'fsdp', axis=0, tiled=True)  208 us
    reduce_scatter x1, waiting for transfers between devices, per_device(): lax.psum_scatter(tile_backward(grad_out, kept_values, rows_list, cols_lis...  163 us
    reduce_scatter x1, waiting for transfers between devices, per_device(): lax.psum_scatter(jnp.einsum('tsk,tsn->skn', picked_x, picked_g, preferred...  120 us
    all_gather x1, waiting for transfers between devices, per_device(): group_rows = lax.all_gather(normed, 'tensor', axis=0, tiled=True)  110 us
    psum x1, blocking collectives, per_device(): grad_gain = lax.psum(gain_part, ('dp', 'fsdp', 'tensor'))  103 us
    psum x1, waiting for transfers between devices, per_device(): grad_tiles = lax.psum(grad_shard, 'dp')  37.8 us
    scatter-add x1, other arithmetic, tile_backward(): placed = jnp.zeros((grad_rows.shape[0], row_tiles, tile_size), jnp.float3...  19.4 us
  transfers between devices with their start and end apart: 5, of which 5 were waited for; matrix products, arithmetic and copies ran while one was open for 3% of the time, Pallas kernels for 0%

commit v1 on v0

--- a/solution.py
+++ b/solution.py
@@ -1,7 +1,19 @@
+import functools
 import jax
 import jax.numpy as jnp
 from jax import lax
 from jax.sharding import PartitionSpec as P
+
+
+def hold_strips_all_by_axis(my_data, dev_axis, mesh_ax):
+    arr_out = lax.psum(my_data, dev_axis)
+    formed = lax.psum(arr_out, mesh_ax)
+    return formed
+
+
+order_pages_here = functools.partial(
+    hold_strips_all_by_axis, dev_axis=("fsdp", "tensor"), mesh_ax="dp"
+)
 
 
 def tile_forward(group_rows, values, rows_list, cols_list, col_tiles):
@@ -68,7 +80,7 @@
     grad_shard = jnp.where(own_held[:, None, None], grad_shard, jnp.zeros_like(grad_shard))
     grad_tiles = lax.psum(grad_shard, "dp")
     gain_part = jnp.sum(input_grad * scaled, axis=0)
-    grad_gain = lax.psum(gain_part, ("dp", "fsdp", "tensor"))
+    grad_gain = order_pages_here(gain_part)
     hidden_grad = input_grad * norm_gain
     grad_x = (
         inv_rms * (hidden_grad - scaled * jnp.mean(hidden_grad * scaled, axis=1, keepdims=True))

time: 849 us -> 2670 us (3.14)
  blocking collectives: 103 us -> 2050 us
  waiting for transfers between devices: 639 us -> 516 us
    psum x1 -> x2, blocking collectives: 103 us -> 2050 us  [the longest x1 1820 us: hold_strips_all_by_axis(): arr_out = lax.psum(my_data, dev_axis)]
    reduce_scatter x1, waiting for transfers between devices: 120 us -> 0.01 us  [per_device(): lax.psum_scatter(jnp.einsum('tsk,tsn->skn', picked_x, picked_g, preferred...]
  transfers between devices with their start and end apart: 5 -> 5, of which waited for: 5 -> 4; matrix products, arithmetic and copies ran while one was open for 3% -> 1% of each run, Pallas kernels for 0% -> 0%
where the time goes in v1:
time: 2670 us
  blocking collectives  2050 us (77%)
  waiting for transfers between devices  516 us (19%)
  other arithmetic  41.6 us (2%)
  local copies, waits for them, and re-layouts  29.9 us (1%)
    psum x1, blocking collectives, hold_strips_all_by_axis(): arr_out = lax.psum(my_data, dev_axis)  1820 us
    psum x1, blocking collectives, hold_strips_all_by_axis(): formed = lax.psum(arr_out, mesh_ax)  227 us
    all_gather x1, waiting for transfers between devices, per_device(): gathered = lax.all_gather(tile_values, 'fsdp', axis=0, tiled=True)  208 us
    reduce_scatter x1, waiting for transfers between devices, per_device(): lax.psum_scatter(tile_backward(grad_out, kept_values, rows_list, cols_lis...  163 us
    all_gather x1, waiting for transfers between devices, per_device(): group_rows = lax.all_gather(normed, 'tensor', axis=0, tiled=True)  110 us
  transfers between devices with their start and end apart: 5, of which 4 were waited for; matrix products, arithmetic and copies ran while one was open for 1% of the time, Pallas kernels for 0%

profile of v1, /device:TPU:1, one launch (start us, length us, event | category | flops | bytes accessed | tf_op | source)
XLA Modules:
  0.0 2668.5 jit_solution(7253578083926251606)
XLA Ops:
  7.2 0.0 all-gather.3.cloned.1.call-start
  7.2 0.7 all-gather.3.cloned.1.call-update
  7.9 0.0 reduce-scatter.7.cloned.1.call-start
  7.9 1.5 copy.32
  9.4 0.6 copy.33
  10.0 0.7 iota_compare_fusion
  10.8 0.1 lt.72
  10.9 0.7 compare_select_fusion
  11.6 0.0 copy-start.4
  11.6 0.0 copy-start.5
  11.6 3.1 gather_fusion.1
  14.6 0.0 copy-done.4
  14.6 0.0 copy-done.5
  14.7 207.7 %all-gather.3.cloned.1.call-done = bf16[64,128,128]{2,1,0:T(8,128)(2,1)} async-done(((bf16[2,128,128]{2,1,0:T(8,128)(2,1)}), bf16[64,128,128]{2,1,0:T(8,128)(2,1)}) %all-gather.3.cloned.1.call-update) | async-done | bytes 2097168 | tf_op jit(solution)/shard_map/all_gather | solution.py:60
  222.3 7.4 fusion.2
  229.8 2.4 broadcast_in_dim.57
  232.2 19.4 scatter_fusion.1
  251.6 2.5 convert_element_type.28
  254.1 2.9 copy.34
  257.0 0.0 copy-start.1
  257.0 0.0 copy-start.2
  257.0 4.1 copy.39
  261.2 0.0 reduce-scatter.7.cloned.1.call-update
  261.2 0.0 all-gather.5.cloned.1.call-start
  261.2 0.0 copy-done.1
  261.3 0.2 fusion.15
  261.4 163.2 %reduce-scatter.7.cloned.1.call-done = bf16[32,4096]{1,0:T(8,128)(2,1)} async-done(((bf16[256,4096]{1,0:T(8,128)(2,1)}), bf16[32,4096]{1,0:T(8,128)(2,1)}) %reduce-scatter.7.cloned.1.call-update) | async-done | bytes 262160 | tf_op jit(solution)/shard_map/reduce_scatter | solution.py:64
  424.6 0.0 copy-done.2
  424.6 1.3 fusion.16
  425.9 1.9 fusion.12
  427.9 0.0 all-gather.5.cloned.1.call-update
  427.9 0.0 reduce-scatter.5.cloned.1.call-start
  428.0 109.9 %all-gather.5.cloned.1.call-done = bf16[256,4096]{1,0:T(8,128)(2,1)} async-done(((bf16[32,4096]{1,0:T(8,128)(2,1)}), bf16[256,4096]{1,0:T(8,128)(2,1)}) %all-gather.5.cloned.1.call-update) | async-done | bytes 2097168 | tf_op jit(solution)/shard_map/all_gather | solution.py:59
  537.8 4.1 copy.29
  541.9 3.2 copy.30
  545.1 3.0 gather_fusion
  548.2 7.0 fusion
  555.2 0.0 copy-start.3
  555.2 0.0 copy-start
  555.2 0.0 reduce-scatter.5.cloned.1.call-update
  555.2 0.0 all-reduce.2.cloned.1.call-start
  555.3 0.6 copy-done.3
  555.8 0.6 constant_dynamic-slice_fusion
  556.4 0.6 iota_compare_fusion.1
  557.1 1818.8 %psum.21 = f32[4096]{0:T(1024)S(1)} all-reduce(f32[4096]{0:T(1024)S(1)} %get-tuple-element.18), channel_id=1, replica_groups=mesh['dp'=2,'fsdp'=32,'tensor'=8] {'fsdp','tensor'}, use_global_device_ids=true, to_apply=%region_6.9 | all-reduce | flops 4096 | bytes 32768 | tf_op jit(solution)/shard_map/psum | solution.py:9
  2375.9 226.6 %psum.22 = f32[4096]{0:T(1024)} all-reduce(f32[4096]{0:T(1024)S(1)} %psum.21), channel_id=1, replica_groups=mesh['dp'=2,'fsdp'=32,'tensor'=8] {'dp'}, use_global_device_ids=true, to_apply=%region_7.10 | all-reduce | flops 4096 | bytes 32768 | tf_op jit(solution)/shard_map/psum | solution.py:10
  2602.6 0.0 reduce-scatter.5.cloned.1.call-done
  2602.6 1.6 broadcast_select_fusion.9
  2604.2 0.0 all-reduce.2.cloned.1.call-update
  2604.2 0.0 copy-done
  2604.2 6.7 fusion.5
  2611.0 0.2 broadcast_in_dim.54
  2611.1 12.4 scatter_fusion
  2623.5 0.2 convert_element_type.26
  2623.7 0.5 copy.31
  2624.2 1.4 copy.37
  2625.6 34.8 %all-reduce.2.cloned.1.call-done = f32[2,128,128]{2,1,0:T(8,128)} async-done(((f32[2,128,128]{2,1,0:T(8,128)}), f32[2,128,128]{2,1,0:T(8,128)}) %all-reduce.2.cloned.1.call-update) | async-done | bytes 131088 | tf_op jit(solution)/shard_map/psum | solution.py:81
  2660.4 1.6 copy.44
  (8 shorter events, 0.0 us)
Async XLA Ops:
  7.2 215.2 %all-gather.3.cloned.1.call-start = ((), (), s32[]{:S(2)}) async-start(), calls=%async_computation.2 | async-start | bytes 2162688 | tf_op jit(solution)/shard_map/all_gather | solution.py:60
  7.9 416.7 %reduce-scatter.7.cloned.1.call-start = ((), (), s32[]{:S(2)}) async-start(), calls=%async_computation.6 | async-start | bytes 2359296 | tf_op jit(solution)/shard_map/reduce_scatter | solution.py:64
  11.6 3.1 copy-start.4
  11.6 3.1 copy-start.5
  257.0 4.2 copy-start.1
  257.0 167.6 %copy-start.2 = (f32[4096]{0:T(1024)S(1)}, f32[4096]{0:T(1024)}, u32[]{:S(2)}) copy-start(f32[4096]{0:T(1024)} %param.12) | copy-start | bytes 49156
  261.2 276.6 %all-gather.5.cloned.1.call-start = ((), (), s32[]{:S(2)}) async-start(), calls=%async_computation.3 | async-start | bytes 2359296 | tf_op jit(solution)/shard_map/all_gather | solution.py:59
  427.9 2174.7 %reduce-scatter.5.cloned.1.call-start = ((), (), s32[]{:S(2)}) async-start(), calls=%async_computation.4 | async-start | bytes 4325376 | tf_op jit(solution)/shard_map/reduce_scatter | solution.py:74
  555.2 0.7 copy-start.3
  555.2 2049.0 %copy-start = (bf16[64,128,128]{2,1,0:T(8,128)(2,1)S(1)}, bf16[64,128,128]{2,1,0:T(8,128)(2,1)}, u32[]{:S(2)}) copy-start(bf16[64,128,128]{2,1,0:T(8,128)(2,1)} %all-gather.3.cloned.1.call-done) | copy-start | bytes 6291460
  555.2 2105.2 %all-reduce.2.cloned.1.call-start = ((), (), s32[]{:S(2)}) async-start(), calls=%async_computation.5 | async-start | bytes 262144 | tf_op jit(solution)/shard_map/psum | solution.py:81
Sparse Core Ops, SparseCore 0:
  10.1 212.2 all-gather.2
  261.3 163.2 reduce-scatter.6
  428.9 108.8 all-gather.4
  555.3 224.9 reduce-scatter.4
  2604.3 56.0 all-reduce.1
